TPU v7x, 256 devices: a whole 4x4x8 slice. The times are simulated.
256 devices in a mesh: row: 16 (over y, x_hi, core), col: 16 (over z, x_lo).
Axes of the slice: x: 4 (x_hi: 2, x_lo: 2; x = x_hi * 2 + x_lo), y: 4, z: 8, core: 2. Of those that a mesh axis runs over, the one named last changes fastest.
Arguments:
- features: bfloat16 [16, 2048, 256], P('col', 'row'), may hold values from -6 to 6
- weight: bfloat16 [256, 256], replicated, may hold values from -0.375 to 0.375
- cotangent: bfloat16 [32768, 256], P(('row', 'col')), may hold values from -6 to 6
- block_vals: bfloat16 [16, 16, 192, 128, 128], P('row', 'col'), may hold values from -0.0625 to 0.0625
- block_slots: int32 [16, 16, 192], P('row', 'col'), may hold values from 0 to 255, as said below
- block_count: int32 [16, 16], P('row', 'col'), may hold values from 1 to 192, as said below
Outputs:
- activated: bfloat16 [32768, 256], P(('row', 'col'))
- grad_features: float32 [16, 2048, 256], P('col', 'row')
Inputs may be any that keep to these rules, and one draw needn't show every extreme that they name: `block_slots`: within one tile the live and the dead slots all name different positions. `block_count`: slots at or past a tile's count are dead and hold arbitrary finite values; some tile is full.
All inputs are finite; a program needn't handle non-finite values.
Results may differ from a plain program's by a relative error of at most 0.0023.
Values may be sent and summed in bfloat16 or wider, within the bound.
A program may use at most 64 MiB of HBM per device.

v0:
```python
import math

import jax
import jax.numpy as jnp
from jax import lax
from jax.sharding import PartitionSpec as P

exact_precision = lax.Precision.HIGHEST


def gelu_tanh_approx(values):
    return jax.nn.gelu(values, approximate=True)


def block_apply(values, slot_ids, live_count, source_nodes, dest_blocks, col_blocks, transposed):
    max_slots = values.shape[0]
    block_size = values.shape[1]
    width = source_nodes.shape[-1]
    wide_source = source_nodes.dtype == jnp.float32
    group_size = math.gcd(max_slots, 32)
    turns = max_slots // group_size
    grouped = values.reshape(turns, group_size, block_size, block_size)
    slot_groups = slot_ids.reshape(turns, group_size)
    slot_rank = jnp.arange(max_slots, dtype=jnp.int32).reshape(turns, group_size)
    source_span_range = jnp.arange(source_nodes.shape[0], dtype=jnp.int32)

    def advance(running, element):
        block_list, position, ranking = element
        if transposed:
            source_idx = position // col_blocks
            dest_idx = position % col_blocks
        else:
            source_idx = position % col_blocks
            dest_idx = position // col_blocks
        if wide_source:
            selector_function = (source_idx[:, None] == source_span_range[None, :]).astype(
                jnp.float32
            )
            selected_entries = jnp.einsum(
                "ld,djk->ljk", selector_function, source_nodes, precision=exact_precision
            )
            block_wide = block_list.astype(jnp.float32)
            product = jnp.einsum(
                "gij,gif->gjf", block_wide, selected_entries, precision=exact_precision
            )
        else:
            selector_function = (source_idx[:, None] == source_span_range[None, :]).astype(
                jnp.bfloat16
            )
            selected_entries = jnp.einsum(
                "ld,djk->ljk", selector_function, source_nodes, preferred_element_type=jnp.float32
            ).astype(jnp.bfloat16)
            product = jnp.einsum(
                "gij,gjf->gif", block_list, selected_entries, preferred_element_type=jnp.float32
            )
        keeping = (ranking < live_count) & (dest_idx >= 0) & (dest_idx < dest_blocks)
        target = jnp.where(keeping, dest_idx, dest_blocks)
        return (running.at[target].add(product, mode="drop"), None)

    start = jnp.zeros((dest_blocks, block_size, width), jnp.float32)
    running, _ = lax.scan(advance, start, (grouped, slot_groups, slot_rank))
    return running


def body(features, weight, cotangent, block_vals, block_slots, block_count):
    values = block_vals[0, 0]
    slot_ids = block_slots[0, 0]
    live_count = block_count[0, 0]
    block_size = values.shape[-1]
    width = features.shape[-1]
    node_rows = features.shape[1]
    row_nodes = node_rows * lax.axis_size("col")
    col_nodes = node_rows * lax.axis_size("row")
    row_blocks = row_nodes // block_size
    col_blocks = col_nodes // block_size
    panel_rows = lax.all_gather(features, "row", axis=1, tiled=True)
    source_nodes = panel_rows.reshape(col_blocks, block_size, width)
    weight_wide = weight.astype(jnp.float32)
    partial_value = block_apply(
        values, slot_ids, live_count, source_nodes, row_blocks, col_blocks, False
    ).reshape(row_nodes, width)
    aggregate = lax.psum_scatter(partial_value, "col", scatter_dimension=0, tiled=True)
    mixed_pre = jnp.dot(aggregate, weight_wide, precision=exact_precision)
    activated_full, pullback = jax.vjp(gelu_tanh_approx, mixed_pre)
    activated = activated_full.astype(jnp.bfloat16)
    grad_pre = pullback(cotangent.astype(jnp.float32))[0]
    grad_agg = jnp.dot(grad_pre, weight_wide.T, precision=exact_precision)
    strip_rows = lax.all_gather(grad_agg, "col", axis=0, tiled=True)
    grad_source = strip_rows.reshape(row_blocks, block_size, width)
    partial_grad = block_apply(
        values, slot_ids, live_count, grad_source, col_blocks, col_blocks, True
    ).reshape(col_nodes, width)
    grad_features = lax.psum_scatter(partial_grad, "row", scatter_dimension=0, tiled=True)
    return (activated, grad_features.reshape(1, node_rows, width))


def solution(mesh):
    return jax.shard_map(
        body,
        mesh=mesh,
        in_specs=(
            P("col", "row", None),
            P(),
            P(("row", "col"), None),
            P("row", "col", None, None, None),
            P("row", "col", None),
            P("row", "col"),
        ),
        out_specs=(P(("row", "col"), None), P("col", "row", None)),
        check_vma=False,
    )
```

profile of v0, /device:TPU:1, one launch (start us, length us, event | category | flops | bytes accessed | tf_op | source)
XLA Modules:
  0.0 492.3 jit_solution(15243606663778344237)
XLA Ops:
  8.5 1.3 reduce.3
  9.9 55.0 %all-gather.3.cloned.1.call-done = bf16[1,2048,256]{2,1,0:T(8,128)(2,1)} async-done(((bf16[1,128,256]{2,1,0:T(8,128)(2,1)}), bf16[1,2048,256]{2,1,0:T(8,128)(2,1)}) %all-gather.3.cloned.1.call-update) | async-done | bytes 1048592 | tf_op jit(solution)/shard_map/all_gather | solution.py:76
  65.1 1.0 copy-done.3
  66.2 75.8 %while.26 = (s32[]{:T(128)}, f32[16,128,256]{2,1,0:T(8,128)S(1)}, s32[6,32]{1,0:T(8,128)S(1)}, s32[]{:T(128)}, s32[6,32]{1,0:T(8,128)S(1)}, /*index=5*/bf16[6,32...) while((s32[]{:T(128)}, f32[16,128,256]{2,1,0:T(8,128)S(1)}, ...), condition=%wide.region_2.3_spmd.clone, body=%wide.region_0.2_spmd.clone.sunk | while | flops 303040096 | bytes 23070176 | solution.py:61
  66.2 0.8 fusion.83
  67.0 4.7 fusion.84
  72.4 6.4 %scatter_fusion = f32[16,128,256]{2,1,0:T(8,128)S(1)} fusion(f32[16,128,256]{2,1,0:T(8,128)S(1)} %get-tuple-element.376, s32[32]{0:T(128)S(1)} %fusion.82, f32[32,128,256]{2,1,0:T(8,128)} %fusion.84), kind=kCustom, calls=%fused_computation.clone.clone.1 | custom fusion | flops 1048576 | bytes 12583040 | tf_op jit(solution)/shard_map/while/body/eval_jaxpr/scatter-add | solution.py:58
  78.8 0.8 fusion.83
  79.7 4.7 fusion.84
  85.1 6.4 %scatter_fusion = f32[16,128,256]{2,1,0:T(8,128)S(1)} fusion(f32[16,128,256]{2,1,0:T(8,128)S(1)} %get-tuple-element.376, s32[32]{0:T(128)S(1)} %fusion.82, f32[32,128,256]{2,1,0:T(8,128)} %fusion.84), kind=kCustom, calls=%fused_computation.clone.clone.1 | custom fusion | flops 1048576 | bytes 12583040 | tf_op jit(solution)/shard_map/while/body/eval_jaxpr/scatter-add | solution.py:58
  92.3 4.7 fusion.84
  97.7 6.4 %scatter_fusion = f32[16,128,256]{2,1,0:T(8,128)S(1)} fusion(f32[16,128,256]{2,1,0:T(8,128)S(1)} %get-tuple-element.376, s32[32]{0:T(128)S(1)} %fusion.82, f32[32,128,256]{2,1,0:T(8,128)} %fusion.84), kind=kCustom, calls=%fused_computation.clone.clone.1 | custom fusion | flops 1048576 | bytes 12583040 | tf_op jit(solution)/shard_map/while/body/eval_jaxpr/scatter-add | solution.py:58
  104.1 0.8 fusion.83
  105.0 4.7 fusion.84
  110.3 6.4 %scatter_fusion = f32[16,128,256]{2,1,0:T(8,128)S(1)} fusion(f32[16,128,256]{2,1,0:T(8,128)S(1)} %get-tuple-element.376, s32[32]{0:T(128)S(1)} %fusion.82, f32[32,128,256]{2,1,0:T(8,128)} %fusion.84), kind=kCustom, calls=%fused_computation.clone.clone.1 | custom fusion | flops 1048576 | bytes 12583040 | tf_op jit(solution)/shard_map/while/body/eval_jaxpr/scatter-add | solution.py:58
  116.8 0.8 fusion.83
  117.6 4.7 fusion.84
  123.0 6.4 %scatter_fusion = f32[16,128,256]{2,1,0:T(8,128)S(1)} fusion(f32[16,128,256]{2,1,0:T(8,128)S(1)} %get-tuple-element.376, s32[32]{0:T(128)S(1)} %fusion.82, f32[32,128,256]{2,1,0:T(8,128)} %fusion.84), kind=kCustom, calls=%fused_computation.clone.clone.1 | custom fusion | flops 1048576 | bytes 12583040 | tf_op jit(solution)/shard_map/while/body/eval_jaxpr/scatter-add | solution.py:58
  129.4 0.8 fusion.83
  130.2 4.7 fusion.84
  135.6 6.4 %scatter_fusion = f32[16,128,256]{2,1,0:T(8,128)S(1)} fusion(f32[16,128,256]{2,1,0:T(8,128)S(1)} %get-tuple-element.376, s32[32]{0:T(128)S(1)} %fusion.82, f32[32,128,256]{2,1,0:T(8,128)} %fusion.84), kind=kCustom, calls=%fused_computation.clone.clone.1 | custom fusion | flops 1048576 | bytes 12583040 | tf_op jit(solution)/shard_map/while/body/eval_jaxpr/scatter-add | solution.py:58
  142.0 1.3 copy-done.2
  143.4 62.8 %reduce-scatter.3.cloned.1.call-done = f32[128,256]{1,0:T(8,128)} async-done(((f32[2048,256]{1,0:T(8,128)}), f32[128,256]{1,0:T(8,128)}) %reduce-scatter.3.cloned.1.call-update) | async-done | bytes 131088 | tf_op jit(solution)/shard_map/reduce_scatter | solution.py:82
  206.3 1.8 multiply_convert_fusion
  208.1 1.0 fusion.33
  209.3 8.6 %copy.8 = bf16[1,1,192,128,128]{3,4,2,1,0:T(8,128)(2,1)} copy(bf16[1,1,192,128,128]{4,3,2,1,0:T(8,128)(2,1)} %bitcast.99) | data formatting | bytes 12582912 | tf_op args[3]
  217.9 65.7 %all-gather.5.cloned.1.call-done = f32[2048,256]{1,0:T(8,128)} async-done(((f32[128,256]{1,0:T(8,128)}), f32[2048,256]{1,0:T(8,128)}) %all-gather.5.cloned.1.call-update) | async-done | bytes 2097168 | tf_op jit(solution)/shard_map/all_gather | solution.py:88
  283.8 116.4 %while.27 = (s32[]{:T(128)}, f32[16,128,256]{2,1,0:T(8,128)S(1)}, s32[6,32]{1,0:T(8,128)S(1)}, s32[]{:T(128)}, s32[6,32]{1,0:T(8,128)S(1)}, /*index=5*/bf16[6,32...) while((s32[]{:T(128)}, f32[16,128,256]{2,1,0:T(8,128)S(1)}, s32[6,32]{1,0:T(8,128)S(1)}, ...), condition=%wide.region_6.7_spmd.clone, body=%wide.region_4.6_spmd.clone.sunk | while | flops 1812989568 | bytes 28313056 | solution.py:61
  283.9 4.3 fusion.90
  288.2 8.0 %fusion.91 = f32[32,128,256]{2,1,0:T(8,128)} fusion(f32[32,128,256]{2,0,1:T(8,128)S(1)} %fusion.90, bf16[6,32,128,128]{2,3,1,0:T(8,128)(2,1)} %get-tuple-element.412, s32[]{:T(128)} %get-tuple-element.399), kind=kOutput, calls=%fused_computation.30.clone.1 | convolution fusion | flops 1610612736 | bytes 9437696 | tf_op jit(solution)/shard_map/while/body/eval_jaxpr/gij,gif->gjf/dot_general | solution.py:43
  296.9 6.4 %scatter_fusion.1 = f32[16,128,256]{2,1,0:T(8,128)S(1)} fusion(f32[16,128,256]{2,1,0:T(8,128)S(1)} %get-tuple-element.400, s32[32]{0:T(128)S(1)} %fusion.89, f32[32,128,256]{2,1,0:T(8,128)} %fusion.91), kind=kCustom, calls=%fused_computation.1.clone.clone.1 | custom fusion | flops 1048576 | bytes 12583040 | tf_op jit(solution)/shard_map/while/body/eval_jaxpr/scatter-add | solution.py:58
  303.3 4.3 fusion.90
  307.6 8.0 %fusion.91 = f32[32,128,256]{2,1,0:T(8,128)} fusion(f32[32,128,256]{2,0,1:T(8,128)S(1)} %fusion.90, bf16[6,32,128,128]{2,3,1,0:T(8,128)(2,1)} %get-tuple-element.412, s32[]{:T(128)} %get-tuple-element.399), kind=kOutput, calls=%fused_computation.30.clone.1 | convolution fusion | flops 1610612736 | bytes 9437696 | tf_op jit(solution)/shard_map/while/body/eval_jaxpr/gij,gif->gjf/dot_general | solution.py:43
  316.3 6.4 %scatter_fusion.1 = f32[16,128,256]{2,1,0:T(8,128)S(1)} fusion(f32[16,128,256]{2,1,0:T(8,128)S(1)} %get-tuple-element.400, s32[32]{0:T(128)S(1)} %fusion.89, f32[32,128,256]{2,1,0:T(8,128)} %fusion.91), kind=kCustom, calls=%fused_computation.1.clone.clone.1 | custom fusion | flops 1048576 | bytes 12583040 | tf_op jit(solution)/shard_map/while/body/eval_jaxpr/scatter-add | solution.py:58
  322.7 4.3 fusion.90
  327.0 8.0 %fusion.91 = f32[32,128,256]{2,1,0:T(8,128)} fusion(f32[32,128,256]{2,0,1:T(8,128)S(1)} %fusion.90, bf16[6,32,128,128]{2,3,1,0:T(8,128)(2,1)} %get-tuple-element.412, s32[]{:T(128)} %get-tuple-element.399), kind=kOutput, calls=%fused_computation.30.clone.1 | convolution fusion | flops 1610612736 | bytes 9437696 | tf_op jit(solution)/shard_map/while/body/eval_jaxpr/gij,gif->gjf/dot_general | solution.py:43
  335.7 6.4 %scatter_fusion.1 = f32[16,128,256]{2,1,0:T(8,128)S(1)} fusion(f32[16,128,256]{2,1,0:T(8,128)S(1)} %get-tuple-element.400, s32[32]{0:T(128)S(1)} %fusion.89, f32[32,128,256]{2,1,0:T(8,128)} %fusion.91), kind=kCustom, calls=%fused_computation.1.clone.clone.1 | custom fusion | flops 1048576 | bytes 12583040 | tf_op jit(solution)/shard_map/while/body/eval_jaxpr/scatter-add | solution.py:58
  342.1 4.3 fusion.90
  346.4 8.0 %fusion.91 = f32[32,128,256]{2,1,0:T(8,128)} fusion(f32[32,128,256]{2,0,1:T(8,128)S(1)} %fusion.90, bf16[6,32,128,128]{2,3,1,0:T(8,128)(2,1)} %get-tuple-element.412, s32[]{:T(128)} %get-tuple-element.399), kind=kOutput, calls=%fused_computation.30.clone.1 | convolution fusion | flops 1610612736 | bytes 9437696 | tf_op jit(solution)/shard_map/while/body/eval_jaxpr/gij,gif->gjf/dot_general | solution.py:43
  355.1 6.4 %scatter_fusion.1 = f32[16,128,256]{2,1,0:T(8,128)S(1)} fusion(f32[16,128,256]{2,1,0:T(8,128)S(1)} %get-tuple-element.400, s32[32]{0:T(128)S(1)} %fusion.89, f32[32,128,256]{2,1,0:T(8,128)} %fusion.91), kind=kCustom, calls=%fused_computation.1.clone.clone.1 | custom fusion | flops 1048576 | bytes 12583040 | tf_op jit(solution)/shard_map/while/body/eval_jaxpr/scatter-add | solution.py:58
  361.5 4.3 fusion.90
  365.8 8.0 %fusion.91 = f32[32,128,256]{2,1,0:T(8,128)} fusion(f32[32,128,256]{2,0,1:T(8,128)S(1)} %fusion.90, bf16[6,32,128,128]{2,3,1,0:T(8,128)(2,1)} %get-tuple-element.412, s32[]{:T(128)} %get-tuple-element.399), kind=kOutput, calls=%fused_computation.30.clone.1 | convolution fusion | flops 1610612736 | bytes 9437696 | tf_op jit(solution)/shard_map/while/body/eval_jaxpr/gij,gif->gjf/dot_general | solution.py:43
  374.5 6.4 %scatter_fusion.1 = f32[16,128,256]{2,1,0:T(8,128)S(1)} fusion(f32[16,128,256]{2,1,0:T(8,128)S(1)} %get-tuple-element.400, s32[32]{0:T(128)S(1)} %fusion.89, f32[32,128,256]{2,1,0:T(8,128)} %fusion.91), kind=kCustom, calls=%fused_computation.1.clone.clone.1 | custom fusion | flops 1048576 | bytes 12583040 | tf_op jit(solution)/shard_map/while/body/eval_jaxpr/scatter-add | solution.py:58
  380.9 4.3 fusion.90
  385.2 8.0 %fusion.91 = f32[32,128,256]{2,1,0:T(8,128)} fusion(f32[32,128,256]{2,0,1:T(8,128)S(1)} %fusion.90, bf16[6,32,128,128]{2,3,1,0:T(8,128)(2,1)} %get-tuple-element.412, s32[]{:T(128)} %get-tuple-element.399), kind=kOutput, calls=%fused_computation.30.clone.1 | convolution fusion | flops 1610612736 | bytes 9437696 | tf_op jit(solution)/shard_map/while/body/eval_jaxpr/gij,gif->gjf/dot_general | solution.py:43
  393.9 6.4 %scatter_fusion.1 = f32[16,128,256]{2,1,0:T(8,128)S(1)} fusion(f32[16,128,256]{2,1,0:T(8,128)S(1)} %get-tuple-element.400, s32[32]{0:T(128)S(1)} %fusion.89, f32[32,128,256]{2,1,0:T(8,128)} %fusion.91), kind=kCustom, calls=%fused_computation.1.clone.clone.1 | custom fusion | flops 1048576 | bytes 12583040 | tf_op jit(solution)/shard_map/while/body/eval_jaxpr/scatter-add | solution.py:58
  400.3 1.3 copy-done.1
  401.6 84.2 %reduce-scatter.5.cloned.1.call-done = f32[128,256]{1,0:T(8,128)} async-done(((f32[2048,256]{1,0:T(8,128)}), f32[128,256]{1,0:T(8,128)}) %reduce-scatter.5.cloned.1.call-update) | async-done | bytes 131088 | tf_op jit(solution)/shard_map/reduce_scatter | solution.py:93
  (45 shorter events, 11.0 us)
Async XLA Ops:
  7.2 199.1 %copy-start = (bf16[256,256]{1,0:T(8,128)(2,1)S(1)}, bf16[256,256]{1,0:T(8,128)(2,1)}, u32[]{:S(2)}) copy-start(bf16[256,256]{1,0:T(8,128)(2,1)} %param.11) | copy-start | bytes 393220
  7.2 57.8 %all-gather.3.cloned.1.call-start = ((), (), s32[]{:S(2)}) async-start(), calls=%async_computation.2 | async-start | bytes 1114112 | tf_op jit(solution)/shard_map/all_gather | solution.py:76
  7.9 198.4 %reduce-scatter.3.cloned.1.call-start = ((), (), s32[]{:S(2)}) async-start(), calls=%async_computation.3 | async-start | bytes 2228224 | tf_op jit(solution)/shard_map/reduce_scatter | solution.py:82
  64.9 1.2 copy-start.3
  142.0 1.3 copy-start.2
  142.0 66.0 %copy-start.4 = (bf16[128,256]{1,0:T(8,128)(2,1)S(1)}, bf16[128,256]{1,0:T(8,128)(2,1)}, u32[]{:S(2)}) copy-start(bf16[128,256]{1,0:T(8,128)(2,1)} %param.12) | copy-start | bytes 196612
  143.4 140.3 %all-gather.5.cloned.1.call-start = ((), (), s32[]{:S(2)}) async-start(), calls=%async_computation.4 | async-start | bytes 2228224 | tf_op jit(solution)/shard_map/all_gather | solution.py:88
  209.1 276.7 %reduce-scatter.5.cloned.1.call-start = ((), (), s32[]{:S(2)}) async-start(), calls=%async_computation.5 | async-start | bytes 2228224 | tf_op jit(solution)/shard_map/reduce_scatter | solution.py:93
  400.3 1.3 copy-start.1
Sparse Core Ops, SparseCore 0:
  10.8 54.1 all-gather.2
  143.5 62.7 reduce-scatter.2
  209.2 74.4 all-gather.4
  401.7 83.9 reduce-scatter.4
where the time goes:
time: 495 us; the launch traced here: 492 us
  waiting for transfers between devices  269 us (54%)
  matrix products  110 us (22%)
  other arithmetic  86 us (17%)
  between operations  13.8 us (3%)
  local copies, waits for them, and re-layouts  13.3 us (3%)
    reduce_scatter x1, waiting for transfers between devices, body(): lax.psum_scatter(partial_grad, 'row', scatter_dimension=0, tiled=True)  84.2 us
    scatter-add x12, other arithmetic, advance(): return (running.at[target].add(product, mode='drop'), None)  76.6 us
    all_gather x1, waiting for transfers between devices, body(): strip_rows = lax.all_gather(grad_agg, 'col', axis=0, tiled=True)  65.7 us
    reduce_scatter x1, waiting for transfers between devices, body(): lax.psum_scatter(partial_value, 'col', scatter_dimension=0, tiled=True)  62.8 us
    all_gather x1, waiting for transfers between devices, body(): panel_rows = lax.all_gather(features, 'row', axis=1, tiled=True)  55 us
    dot_general x6, matrix products, advance(): jnp.einsum('gij,gif->gjf', block_wide, selected_entries, precision=exact_...  47.8 us
    dot_general x6, matrix products, advance(): jnp.einsum('gij,gjf->gif', block_list, selected_entries, preferred_elemen...  28.3 us
    dot_general x6, matrix products, advance(): jnp.einsum('ld,djk->ljk', selector_function, source_nodes, precision=exac...  26.1 us
  transfers between devices with their start and end apart: 4, of which 4 were waited for; matrix products, arithmetic and copies ran while one was open for 2% of the time, Pallas kernels for 0%

commit v1 on v0

v1 whole, which is shorter than its diff:
```python
import jax
import jax.numpy as jnp
from jax import lax
from jax.experimental import pallas as pl
from jax.experimental.pallas import tpu as pltpu
from jax.sharding import PartitionSpec as P

MESH = pl.DeviceIdType.MESH
BLK = 128
F = 256
SLOTS = 192
NB = 16
NZ = 8
NY = 4
F32 = jnp.float32
BF16 = jnp.bfloat16
LEVELS = 32700.0
N_COPIES = 88
N_LOADS = 4
ROOT = 0.7978845608028654


def power(e):
    return jnp.exp2(e)


def quant(v, dst):
    rows = v.shape[0]
    top = jnp.maximum(jnp.max(jnp.abs(v), axis=0, keepdims=True), 1e-30)
    e = jnp.ceil(jnp.log2(top) + 0.001)
    q = jnp.round(v * (LEVELS * power(-e)))
    dst[0:rows, :] = q.astype(jnp.int32).astype(jnp.int16)
    dst[rows : rows + 16, :] = jnp.broadcast_to(e, (16, v.shape[1])).astype(jnp.int32).astype(jnp.int16)


def dequant(src, rows):
    e = src[rows : rows + 16, :].astype(jnp.int32)[0:1, :].astype(F32)
    return src[0:rows, :].astype(jnp.int32).astype(F32) * (power(e) * (1.0 / LEVELS))


def split3(v):
    hi = v.astype(BF16)
    rest = v - hi.astype(F32)
    mid = rest.astype(BF16)
    lo = (rest - mid.astype(F32)).astype(BF16)
    return jnp.concatenate([hi, mid, lo], axis=0)


def kernel(
    feat, weight, cot, vals_hbm, inv,
    act, gfeat,
    vals, dense, xall, part, gt, qsum,
    h0s, h0r, h0s0, h0r0, h1s, h1r, h1s0, h1r0, xs, xr,
    sibr, ys, yr, ds, dr, tsum,
    send_sem, recv_sem, load_sem,
):
    row = lax.axis_index("row")
    col = lax.axis_index("col")
    core = row % 2
    xh = (row // 2) % 2
    y = row // 4
    z = col // 2
    xl = col % 2
    d = 1 - 2 * core

    def rid(yy, xx, cc):
        return ((yy + 2 * NY) % NY) * 4 + xx * 2 + cc

    def zmod(zz):
        return (zz + 2 * NZ) % NZ

    to_yp = (rid(y + d, xh, core), col)
    to_ym = (rid(y - d, xh, core), col)
    to_xh = (rid(y, 1 - xh, core), col)
    to_sib = (rid(y, xh, 1 - core), col)
    to_zp = (row, zmod(z + 1) * 2 + xl)
    to_zm = (row, zmod(z - 1) * 2 + xl)
    to_xl = (row, z * 2 + 1 - xl)

    copies = []

    def push(src, dst, dev):
        i = len(copies)
        c = pltpu.make_async_remote_copy(
            src_ref=src, dst_ref=dst, send_sem=send_sem.at[i], recv_sem=recv_sem.at[i],
            device_id=dev, device_id_type=MESH,
        )
        c.start()
        copies.append(c)
        return c

    loads = []
    step = SLOTS // N_LOADS
    for i in range(N_LOADS):
        c = pltpu.make_async_copy(vals_hbm.at[pl.ds(i * step, step)], vals.at[pl.ds(i * step, step)], load_sem.at[i])
        c.start()
        loads.append(c)

    barrier = pltpu.get_barrier_semaphore()
    for dev in (to_yp, to_ym, to_xh, to_sib, to_zp, to_zm, to_xl):
        pl.semaphore_signal(barrier, inc=1, device_id=dev, device_id_type=MESH)

    def xat(r):
        return xall.at[pl.ds(pl.multiple_of(r * BLK, BLK), BLK)]

    xat(row)[...] = feat[0]
    vals[SLOTS] = jnp.zeros((BLK, BLK), BF16)
    pl.semaphore_wait(barrier, 7)

    def put(r, dev):
        return push(xat(r), xat(r), dev)

    r_x = rid(y, 1 - xh, core)
    r_m = rid(y - d, xh, core)
    r_p = rid(y + d, xh, core)
    r_mx = rid(y - d, 1 - xh, core)
    r_px = rid(y + d, 1 - xh, core)
    r_o = rid(y + 2, xh, core)
    r_ox = rid(y + 2, 1 - xh, core)
    a_x = put(row, to_xh)
    a_p = put(row, to_yp)
    a_m = put(row, to_ym)
    sib = [put(row, to_sib)]

    def build(lo, hi):
        def one(r, carry):
            for c in range(NB):
                dense[pl.ds(pl.multiple_of(r * BLK, BLK), BLK), c * BLK : (c + 1) * BLK] = vals[inv[r * NB + c]]
            return carry

        lax.fori_loop(lo, hi, one, 0)

    a_p.wait_recv()
    a_o = put(r_m, to_yp)
    a_x.wait_recv()
    a_px = put(r_x, to_yp)
    a_mx = put(r_x, to_ym)
    sib.append(put(r_m, to_sib))
    sib.append(put(r_x, to_sib))
    a_m.wait_recv()
    sib.append(put(r_p, to_sib))
    for c in loads:
        c.wait()
    build(0, 6)
    a_px.wait_recv()
    a_ox = put(r_mx, to_yp)
    a_o.wait_recv()
    sib.append(put(r_mx, to_sib))
    sib.append(put(r_o, to_sib))
    build(6, 11)
    a_mx.wait_recv()
    sib.append(put(r_px, to_sib))
    build(11, 16)
    a_ox.wait_recv()
    sib.append(put(r_ox, to_sib))
    for c in sib:
        c.wait_recv()

    targets = [z + 4, z + 3, z - 3, z + 2, z - 2, z + 1, z - 1, z]
    own_rows = pl.ds(pl.multiple_of(xl * BLK, BLK), BLK)
    far_rows = pl.ds(pl.multiple_of((1 - xl) * BLK, BLK), BLK)
    x_copy = {}

    def forward(i):
        t = zmod(targets[i])
        part[i] = jnp.dot(
            dense[pl.ds(pl.multiple_of(t * 2 * BLK, 2 * BLK), 2 * BLK), :], xall[...], preferred_element_type=F32
        )
        quant(part[i, far_rows, BLK:F], xs.at[i])
        x_copy[i] = push(xs.at[i], xr.at[i], to_xl)

    forward(0)
    quant(part[0, 0:BLK, 0:BLK], h0s0.at[0])
    h0p = push(h0s0.at[0], h0r0.at[0], to_zp)
    quant(part[0, BLK : 2 * BLK, 0:BLK], h0s0.at[1])
    h0m = push(h0s0.at[1], h0r0.at[1], to_zm)
    forward(1)
    forward(2)

    def mine(i):
        x_copy[i].wait_recv()
        return part[i, own_rows, BLK:F] + dequant(xr.at[i], BLK)

    first = mine(0)
    quant(first[0:64], h1s0.at[0])
    h1p = push(h1s0.at[0], h1r0.at[0], to_zp)
    quant(first[64:128], h1s0.at[1])
    h1m = push(h1s0.at[1], h1r0.at[1], to_zm)

    def chain0(s, way, i, copy, dev):
        copy.wait_recv()
        out = h0s.at[way, s]
        if s == 0:
            got = dequant(h0r0.at[way], BLK)
            kept = part[i, :, 0:BLK]
            if way == 0:
                v = jnp.concatenate([kept[0:BLK] + got, kept[BLK : 2 * BLK]], axis=0)
            else:
                v = jnp.concatenate([kept[0:BLK], kept[BLK : 2 * BLK] + got], axis=0)
        else:
            v = part[i, :, 0:BLK] + dequant(h0r.at[way, s - 1], 2 * BLK)
        quant(v, out)
        return push(out, h0r.at[way, s], dev)

    def chain1(s, way, i, copy, dev):
        kept = mine(i)
        copy.wait_recv()
        out = h1s.at[way, s]
        if s == 0:
            got = dequant(h1r0.at[way], 64)
            if way == 0:
                v = jnp.concatenate([kept[0:64] + got, kept[64:128]], axis=0)
            else:
                v = jnp.concatenate([kept[0:64], kept[64:128] + got], axis=0)
        else:
            v = kept + dequant(h1r.at[way, s - 1], BLK)
        quant(v, out)
        return push(out, h1r.at[way, s], dev)

    for s in range(3):
        h0p = chain0(s, 0, 1 + 2 * s, h0p, to_zp)
        h0m = chain0(s, 1, 2 + 2 * s, h0m, to_zm)
        if s < 2:
            forward(3 + 2 * s)
            forward(4 + 2 * s)
        else:
            forward(7)
        h1p = chain1(s, 0, 1 + 2 * s, h1p, to_zp)
        h1m = chain1(s, 1, 2 + 2 * s, h1m, to_zm)

    h0p.wait_recv()
    h0m.wait_recv()
    part[7, :, 0:BLK] = part[7, :, 0:BLK] + dequant(h0r.at[0, 2], 2 * BLK) + dequant(h0r.at[1, 2], 2 * BLK)
    quant(part[7, far_rows, 0:BLK], xs.at[8])
    x_last = push(xs.at[8], xr.at[8], to_xl)
    right = mine(7)
    h1p.wait_recv()
    h1m.wait_recv()
    right = right + dequant(h1r.at[0, 2], BLK) + dequant(h1r.at[1, 2], BLK)
    x_last.wait_recv()
    left = part[7, own_rows, 0:BLK] + dequant(xr.at[8], BLK)
    agg = jnp.concatenate([left, right], axis=1)

    w = weight[...]
    three = jnp.dot(split3(agg), w, preferred_element_type=F32)
    v = three[0:BLK] + three[BLK : 2 * BLK] + three[2 * BLK : 3 * BLK]
    v2 = v * v
    th = jnp.tanh(ROOT * (v + 0.044715 * (v2 * v)))
    act[...] = (0.5 * v * (1.0 + th)).astype(BF16)
    slope = 0.5 * (1.0 + th) + (0.5 * ROOT) * v * (1.0 - th * th) * (1.0 + 3 * 0.044715 * v2)
    grad_pre = cot[...].astype(F32) * slope
    tri = lax.dot_general(w, split3(grad_pre), (((1,), (1,)), ((), ())), preferred_element_type=F32)
    gt[col] = (tri[:, 0:BLK] + tri[:, BLK : 2 * BLK] + tri[:, 2 * BLK : 3 * BLK]).astype(BF16)

    def spot(zz, lane, lo, hi):
        return gt.at[zmod(zz) * 2 + lane, lo:hi]

    def send(zz, lane, lo, hi, dev):
        return push(spot(zz, lane, lo, hi), spot(zz, lane, lo, hi), dev)

    far = 1 - xl
    x0 = send(z, xl, 0, BLK, to_xl)
    op = send(z, xl, 0, F, to_zp)
    om = send(z, xl, 0, F, to_zm)
    xf = {0: [send(z, xl, BLK, F, to_xl)]}
    x0.wait_recv()
    pp = send(z, far, 0, BLK, to_zp)
    pm = send(z, far, 0, BLK, to_zm)

    def product(zz, n):
        t = zmod(zz)
        lhs = jnp.concatenate([gt[t * 2], gt[t * 2 + 1]], axis=1)
        rhs = dense[pl.ds(pl.multiple_of(t * 2 * BLK, 2 * BLK), 2 * BLK), pl.ds(pl.multiple_of(n * 2 * BLK, 2 * BLK), 2 * BLK)]
        return jnp.dot(lhs, rhs, preferred_element_type=F32)

    def add_pass(zs, fresh):
        def one(n, carry):
            total = product(zs[0], n)
            for zz in zs[1:]:
                total = total + product(zz, n)
            if fresh:
                qsum[2 * n] = total[:, 0:BLK]
                qsum[2 * n + 1] = total[:, BLK:F]
            else:
                qsum[2 * n] = qsum[2 * n] + total[:, 0:BLK]
                qsum[2 * n + 1] = qsum[2 * n + 1] + total[:, BLK:F]
            return carry

        lax.fori_loop(0, NB // 2, one, 0)

    for s in range(1, 4):
        op.wait_recv()
        om.wait_recv()
        if s < 3:
            op = send(z - s, xl, 0, F, to_zp)
            om = send(z + s, xl, 0, F, to_zm)
        else:
            op = send(z - s, xl, 0, BLK, to_zp)
            om = send(z + s, xl, BLK, F, to_zm)
        xf[s] = [send(z - s, xl, BLK, F, to_xl), send(z + s, xl, BLK, F, to_xl)]
        pp.wait_recv()
        pm.wait_recv()
        if s < 3:
            pp = send(z - s, far, 0, BLK, to_zp)
            pm = send(z + s, far, 0, BLK, to_zm)
        else:
            pp = send(z - s, far, 0, 64, to_zp)
            pm = send(z + s, far, 64, BLK, to_zm)
        for c in xf[s - 1]:
            c.wait_recv()
        add_pass([z] if s == 1 else [z - s + 1, z + s - 1], s == 1)
    om.wait_recv()
    op.wait_recv()
    xf[4] = [send(z + 4, xl, BLK, F, to_xl)]
    for c in xf[3]:
        c.wait_recv()
    add_pass([z - 3, z + 3], False)
    pp.wait_recv()
    pm.wait_recv()
    xf[4][0].wait_recv()

    order = [(y + 2, 0), (y + 2, 1), (y + 1, 0), (y + 1, 1), (y - 1, 0), (y - 1, 1), (y, 0), (y, 1)]
    from_sib = []
    for i, (yy, xx) in enumerate(order):
        n = ((yy + 2 * NY) % NY) * 2 + xx
        total = product(z + 4, n)
        qsum[2 * n] = qsum[2 * n] + total[:, 0:BLK]
        qsum[2 * n + 1] = qsum[2 * n + 1] + total[:, BLK:F]
        from_sib.append(push(qsum.at[2 * n + 1 - core], sibr.at[n], to_sib))

    def pair(yy, xx):
        n = ((yy + 2 * NY) % NY) * 2 + xx
        return qsum[2 * n + core] + sibr[n]

    for c in from_sib[0:2]:
        c.wait_recv()
    for k in range(2):
        quant(pair(y + 2, k), ys.at[0, k])
    y1 = push(ys.at[0], yr.at[0], to_yp)
    for c in from_sib[2:6]:
        c.wait_recv()
    for k in range(2):
        quant(pair(y - d, k), ys.at[1, k])
    y2 = push(ys.at[1], yr.at[1], to_ym)
    for k in range(2):
        tsum[k] = pair(y + d, k)
    y1.wait_recv()
    for k in range(2):
        quant(tsum[k] + dequant(yr.at[0, k], F), ys.at[2, k])
    y3 = push(ys.at[2], yr.at[2], to_yp)
    for c in from_sib[6:8]:
        c.wait_recv()
    for k in range(2):
        tsum[k] = pair(y, k)
    y2.wait_recv()
    y3.wait_recv()
    for k in range(2):
        tsum[k] = tsum[k] + dequant(yr.at[1, k], F) + dequant(yr.at[2, k], F)
    quant(tsum[1 - xh], ds)
    last = push(ds, dr, to_xh)
    last.wait_recv()
    gfeat[0] = (tsum[xh] + dequant(dr, F)).T

    for c in copies:
        c.wait_send()


def body(features, weight, cotangent, block_vals, block_slots, block_count):
    slots = block_slots[0, 0]
    ids = lax.broadcasted_iota(jnp.int32, (SLOTS, NB * NB), 0)
    place = lax.broadcasted_iota(jnp.int32, (SLOTS, NB * NB), 1)
    hit = (slots[:, None] == place) & (ids < block_count[0, 0])
    inv = SLOTS - jnp.sum(jnp.where(hit, SLOTS - ids, 0), axis=0, dtype=jnp.int32)
    vm = pl.BlockSpec(memory_space=pltpu.VMEM)
    i16 = jnp.int16
    v = pltpu.VMEM
    return pl.pallas_call(
        kernel,
        out_shape=(
            jax.ShapeDtypeStruct((BLK, F), BF16),
            jax.ShapeDtypeStruct((1, BLK, F), F32),
        ),
        in_specs=[vm, vm, vm, pl.BlockSpec(memory_space=pl.ANY), pl.BlockSpec(memory_space=pltpu.SMEM)],
        out_specs=(vm, vm),
        scratch_shapes=[
            v((SLOTS + 1, BLK, BLK), BF16),
            v((NB * BLK, NB * BLK), BF16),
            v((NB * BLK, F), BF16),
            v((8, 2 * BLK, F), F32),
            v((NB, F, BLK), BF16),
            v((NB, F, BLK), F32),
            v((2, 3, 2 * BLK + 16, BLK), i16),
            v((2, 3, 2 * BLK + 16, BLK), i16),
            v((2, BLK + 16, BLK), i16),
            v((2, BLK + 16, BLK), i16),
            v((2, 3, BLK + 16, BLK), i16),
            v((2, 3, BLK + 16, BLK), i16),
            v((2, 80, BLK), i16),
            v((2, 80, BLK), i16),
            v((9, BLK + 16, BLK), i16),
            v((9, BLK + 16, BLK), i16),
            v((8, F, BLK), F32),
            v((3, 2, F + 16, BLK), i16),
            v((3, 2, F + 16, BLK), i16),
            v((F + 16, BLK), i16),
            v((F + 16, BLK), i16),
            v((2, F, BLK), F32),
            pltpu.SemaphoreType.DMA((N_COPIES,)),
            pltpu.SemaphoreType.DMA((N_COPIES,)),
            pltpu.SemaphoreType.DMA((N_LOADS,)),
        ],
        compiler_params=pltpu.CompilerParams(
            collective_id=0, has_side_effects=True, vmem_limit_bytes=48 * 1024 * 1024
        ),
        name="layer",
    )(features, weight, cotangent, block_vals.reshape(SLOTS, BLK, BLK), inv)


def solution(mesh):
    return jax.shard_map(
        body,
        mesh=mesh,
        in_specs=(
            P("col", "row", None),
            P(),
            P(("row", "col"), None),
            P("row", "col", None, None, None),
            P("row", "col", None),
            P("row", "col"),
        ),
        out_specs=(P(("row", "col"), None), P("col", "row", None)),
        check_vma=False,
    )
```

time: 495 us -> 83 us (0.17)
  the two profiles are of different devices: /device:TPU:1 before, /device:TPU:2 now
where the time goes in v1:
time: 83 us; the launch traced here: 82.8 us
  Pallas kernels  76.8 us (93%)
  local copies, waits for them, and re-layouts  3.86 us (5%)
  between operations  1.31 us (2%)
  other arithmetic  0.85 us (1%)
    pallas_call x1, Pallas kernels, body(): pl.pallas_call(kernel, out_shape=(jax.ShapeDtypeStruct((BLK, F), BF16), j...  76.8 us
    unnamed x8, local copies, waits for them, and re-layouts  3.86 us

profile of v1, /device:TPU:2, one launch (start us, length us, event | category | flops | bytes accessed | tf_op | source)
XLA Modules:
  0.0 82.8 jit_solution(18086959170695663249)
XLA Ops:
  1.3 0.8 %select_reduce_fusion = s32[256]{0:T(256)S(1)} fusion(s32[192]{0:T(256)S(1)} %iota_subtract_fusion, s32[192]{0:T(256)} %bitcast.5, pred[192]{0:T(512)(128)(4,1)S(1)} %iota_compare_fusion.1), kind=kLoop, calls=%fused_computation | loop fusion | flops 196352 | bytes 2752 | tf_op jit(solution)/shard_map/reduce_sum | solution.py:373
  2.1 0.0 copy-start
  2.2 0.9 %copy-done = bf16[256,256]{1,0:T(8,128)(2,1)S(1)} copy-done((bf16[256,256]{1,0:T(8,128)(2,1)S(1)}, bf16[256,256]{1,0:T(8,128)(2,1)}, u32[]{:S(2)}) %copy-start) | copy-done | bytes 131096
  3.1 0.0 copy-start.1
  3.1 0.8 %copy-done.1 = bf16[1,128,256]{2,1,0:T(8,128)(2,1)S(1)} copy-done((bf16[1,128,256]{2,1,0:T(8,128)(2,1)S(1)}, bf16[1,128,256]{2,1,0:T(8,128)(2,1)}, u32[]{:S(2)}) %copy-start.1) | copy-done | bytes 65560
  3.9 0.0 copy-start.2
  3.9 0.8 %copy-done.2 = bf16[128,256]{1,0:T(8,128)(2,1)S(1)} copy-done((bf16[128,256]{1,0:T(8,128)(2,1)S(1)}, bf16[128,256]{1,0:T(8,128)(2,1)}, u32[]{:S(2)}) %copy-start.2) | copy-done | bytes 65560
  4.7 76.8 %layer.1 = (bf16[128,256]{1,0:T(8,128)(2,1)S(1)}, f32[1,128,256]{2,1,0:T(8,128)S(1)}) custom-call(bf16[1,128,256]{2,1,0:T(8,128)(2,1)S(1)} %copy-done.1, bf16[256,256]{1,0:T(8,128)(2,1)S(1)} %copy-done, bf16[128,256]{1,0:T(8,128)(2,1)S(1)} %copy-done.2, bf16[192,128,128]{2,1,0:T(8,128)(2,1)} %bitcast.4, s32[256]{0:T(256)S(1)} %broadcast_subtract_fusion.inv), custom_call_target="tpu_custom_call" | custom-call | tf_op jit(solution)/shard_map/layer/pallas_call | solution.py:377
  81.5 0.6 copy.11
  82.2 0.7 copy.12
  (3 shorter events, 0.0 us)
Async XLA Ops:
  2.1 0.9 %copy-start = (bf16[256,256]{1,0:T(8,128)(2,1)S(1)}, bf16[256,256]{1,0:T(8,128)(2,1)}, u32[]{:S(2)}) copy-start(bf16[256,256]{1,0:T(8,128)(2,1)} %weight.1) | copy-start | bytes 393220
  3.1 0.8 %copy-start.1 = (bf16[1,128,256]{2,1,0:T(8,128)(2,1)S(1)}, bf16[1,128,256]{2,1,0:T(8,128)(2,1)}, u32[]{:S(2)}) copy-start(bf16[1,128,256]{2,1,0:T(8,128)(2,1)} %feat.1) | copy-start | bytes 196612
  3.9 0.8 %copy-start.2 = (bf16[128,256]{1,0:T(8,128)(2,1)S(1)}, bf16[128,256]{1,0:T(8,128)(2,1)}, u32[]{:S(2)}) copy-start(bf16[128,256]{1,0:T(8,128)(2,1)} %cot.1) | copy-start | bytes 196612

commit v2 on v0

v2 whole, which is shorter than its diff:
```python
import jax
import jax.numpy as jnp
from jax import lax
from jax.experimental import pallas as pl
from jax.experimental.pallas import tpu as pltpu
from jax.sharding import PartitionSpec as P

MESH = pl.DeviceIdType.MESH
BLK = 128
F = 256
SLOTS = 192
NB = 16
NZ = 8
NY = 4
F32 = jnp.float32
BF16 = jnp.bfloat16
LEVELS = 32700.0
N_COPIES = 96
N_LOADS = 4
ROOT = 0.7978845608028654


def quant(v, dst):
    rows = v.shape[0]
    top = jnp.maximum(jnp.max(jnp.abs(v), axis=0, keepdims=True), 1e-30)
    e = jnp.ceil(jnp.log2(top) + 0.001)
    q = jnp.round(v * (LEVELS * jnp.exp2(-e)))
    dst[0:rows, :] = q.astype(jnp.int32).astype(jnp.int16)
    dst[rows : rows + 16, :] = jnp.broadcast_to(e, (16, v.shape[1])).astype(jnp.int32).astype(jnp.int16)


def dequant(src):
    rows = src.shape[0] - 16
    e = src[rows : rows + 16, :].astype(jnp.int32)[0:1, :].astype(F32)
    return src[0:rows, :].astype(jnp.int32).astype(F32) * (jnp.exp2(e) * (1.0 / LEVELS))


def split3(v):
    hi = v.astype(BF16)
    rest = v - hi.astype(F32)
    mid = rest.astype(BF16)
    lo = (rest - mid.astype(F32)).astype(BF16)
    return jnp.concatenate([hi, mid, lo], axis=0)


def kernel(
    feat_hbm, weight_hbm, cot_hbm, vals_hbm, slots_hbm, count,
    act, gfeat,
    weight, cot, slots, inv_v, inv, vals, dense, xall, part, gt, qsum,
    xs, xr, ns, nr, fs, fr, ms, mr, es, er, sibr, ds, dr,
    send_sem, recv_sem, load_sem,
):
    row = lax.axis_index("row")
    col = lax.axis_index("col")
    core = row % 2
    xh = (row // 2) % 2
    y = row // 4
    z = col // 2
    xl = col % 2

    def rid(yy, xx, cc):
        return ((yy + 2 * NY) % NY) * 4 + xx * 2 + cc

    def zmod(zz):
        return (zz + 2 * NZ) % NZ

    def swap(b, k):
        return 1 - b if k else b

    row_moves = [(2, 1), (1, 1), (-1, 1), (2, 0), (0, 1), (1, 0), (-1, 0)]
    row_devs = [(rid(y + dy, swap(xh, dx), core), col) for dy, dx in row_moves]
    z_devs = [(row, zmod(z + dz) * 2 + xl) for dz in (2, -2, 1, -1)]
    to_sib = (rid(y, xh, 1 - core), col)
    to_xl = (row, z * 2 + 1 - xl)

    copies = []

    def push(src, dst, dev):
        i = len(copies)
        c = pltpu.make_async_remote_copy(
            src_ref=src, dst_ref=dst, send_sem=send_sem.at[i], recv_sem=recv_sem.at[i],
            device_id=dev, device_id_type=MESH,
        )
        c.start()
        copies.append(c)
        return c

    barrier = pltpu.get_barrier_semaphore()
    for dev in row_devs + z_devs + [to_sib, to_xl]:
        pl.semaphore_signal(barrier, inc=1, device_id=dev, device_id_type=MESH)

    def xat(r):
        return xall.at[pl.ds(pl.multiple_of(r * BLK, BLK), BLK)]

    loads = []

    def load(src, dst):
        c = pltpu.make_async_copy(src, dst, load_sem.at[len(loads)])
        c.start()
        loads.append(c)

    load(feat_hbm.at[0], xat(row))
    load(slots_hbm.at[0], slots)
    step = SLOTS // N_LOADS
    for i in range(N_LOADS):
        load(vals_hbm.at[pl.ds(i * step, step)], vals.at[pl.ds(i * step, step)])
    load(weight_hbm, weight)
    load(cot_hbm, cot)
    vals[SLOTS] = jnp.zeros((BLK, BLK), BF16)
    loads[1].wait()
    place = lax.broadcasted_iota(jnp.int32, (NB * NB, SLOTS), 0)
    ids = lax.broadcasted_iota(jnp.int32, (NB * NB, SLOTS), 1)
    hit = jnp.where((slots[...] == place) & (ids < count[0, 0]), 1.0, 0.0).astype(BF16)
    marks = (SLOTS - lax.broadcasted_iota(jnp.int32, (8, SLOTS), 1)).astype(F32).astype(BF16)
    found = lax.dot_general(marks, hit, (((1,), (1,)), ((), ())), preferred_element_type=F32)
    inv_v[...] = SLOTS - found.astype(jnp.int32)
    to_smem = pltpu.make_async_copy(inv_v, inv, load_sem.at[len(loads)])
    to_smem.start()
    loads[0].wait()
    pl.semaphore_wait(barrier, len(row_devs) + len(z_devs) + 2)

    def put(r, dev):
        return push(xat(r), xat(r), dev)

    feats = [put(row, dev) for dev in row_devs]
    sib = [put(row, to_sib)]

    def build(lo, hi):
        def one(r, carry):
            for c in range(NB):
                dense[pl.ds(pl.multiple_of(r * BLK, BLK), BLK), c * BLK : (c + 1) * BLK] = vals[jnp.clip(inv[0, r * NB + c], 0, SLOTS)]
            return carry

        lax.fori_loop(lo, hi, one, 0)

    to_smem.wait()
    for c in loads[2:]:
        c.wait()
    build(0, NB)
    for i in (5, 6, 4, 3, 1, 2, 0):
        dy, dx = row_moves[i]
        feats[i].wait_recv()
        sib.append(put(rid(y - dy, swap(xh, dx), core), to_sib))
    for c in sib:
        c.wait_recv()

    own_rows = pl.ds(pl.multiple_of(xl * BLK, BLK), BLK)
    far_rows = pl.ds(pl.multiple_of((1 - xl) * BLK, BLK), BLK)
    moves = [4, 3, -3, 1, -1, 2, -2, 0]
    to_z = {k: (row, zmod(z + k) * 2 + xl) for k in (1, -1, 2, -2)}
    half = [slice(0, BLK), slice(BLK, F)]
    x_copy = {}
    near = {}

    def forward(i):
        t = zmod(z + moves[i])
        part[i] = jnp.dot(
            dense[pl.ds(pl.multiple_of(t * 2 * BLK, 2 * BLK), 2 * BLK), :], xall[...], preferred_element_type=F32
        )

    def cross(i, h):
        quant(part[i, far_rows, half[h]], xs.at[h, i])
        x_copy[i, h] = push(xs.at[h, i], xr.at[h, i], to_xl)

    def joined(i, h):
        x_copy[i, h].wait_recv()
        return part[i, own_rows, half[h]] + dequant(xr.at[h, i])

    def pass_on(v, src, dst, dev):
        quant(v, src)
        return push(src, dst, dev)

    for i in range(8):
        forward(i)
        if i in (3, 4):
            for h in range(2):
                near[i - 3, h] = pass_on(part[i, :, half[h]], ns.at[h, i - 3], nr.at[h, i - 3], to_z[moves[i]])
        elif i < 7:
            cross(i, 0)
        if i == 5:
            cross(0, 1)
            cross(1, 1)
    for i in (2, 5, 6):
        cross(i, 1)
    four = {}
    three = {}
    for h in range(2):
        four[h] = pass_on(joined(0, h), fs.at[h], fr.at[h], to_z[2 - 4 * h])
        for k in range(2):
            three[k, h] = pass_on(joined(1 + k, h), ms.at[h, k], mr.at[h, k], to_z[1 - 2 * k])
        if h == 0:
            for k in range(4):
                near[k % 2, k // 2].wait_recv()
            for q in range(2):
                part[7, :, half[q]] = part[7, :, half[q]] + dequant(nr.at[q, 0]) + dequant(nr.at[q, 1])
                cross(7, q)
    last = {}
    for h in range(2):
        for k in range(2):
            v = joined(5 + k, h)
            three[k, h].wait_recv()
            v = v + dequant(mr.at[h, k])
            if h == k:
                four[h].wait_recv()
                v = v + dequant(fr.at[h])
            last[k, h] = pass_on(v, es.at[h, k], er.at[h, k], to_z[2 - 4 * k])
    total = []
    for h in range(2):
        v = joined(7, h)
        for k in range(2):
            last[k, h].wait_recv()
            v = v + dequant(er.at[h, k])
        total.append(v)
    agg = jnp.concatenate(total, axis=1)

    w = weight[...]
    three = jnp.dot(split3(agg), w, preferred_element_type=F32)
    v = three[0:BLK] + three[BLK : 2 * BLK] + three[2 * BLK : 3 * BLK]
    v2 = v * v
    th = jnp.tanh(ROOT * (v + 0.044715 * (v2 * v)))
    act[...] = (0.5 * v * (1.0 + th)).astype(BF16)
    slope = 0.5 * (1.0 + th) + (0.5 * ROOT) * v * (1.0 - th * th) * (1.0 + 3 * 0.044715 * v2)
    grad_pre = cot[...].astype(F32) * slope
    tri = lax.dot_general(w, split3(grad_pre), (((1,), (1,)), ((), ())), preferred_element_type=F32)
    gt[col] = (tri[:, 0:BLK] + tri[:, BLK : 2 * BLK] + tri[:, 2 * BLK : 3 * BLK]).astype(BF16)

    far = 1 - xl

    def send(zz, lane, h, dev):
        spot = gt.at[zmod(zz) * 2 + lane, half[h]]
        return push(spot, spot, dev)

    g = {}
    for h in range(2):
        for k in (2, -2):
            g[k, h] = send(z, xl, h, to_z[k])
        g[0, h] = send(z, xl, h, to_xl)
        for k in (1, -1):
            g[k, h] = send(z, xl, h, to_z[k])

    def product(zz, n):
        t = zmod(zz)
        lhs = jnp.concatenate([gt[t * 2], gt[t * 2 + 1]], axis=1)
        rhs = dense[pl.ds(pl.multiple_of(t * 2 * BLK, 2 * BLK), 2 * BLK), pl.ds(pl.multiple_of(n * 2 * BLK, 2 * BLK), 2 * BLK)]
        return jnp.dot(lhs, rhs, preferred_element_type=F32)

    def add_to(zs_, n, fresh):
        total = product(zs_[0], n)
        for zz in zs_[1:]:
            total = total + product(zz, n)
        if fresh:
            qsum[2 * n] = total[:, 0:BLK]
            qsum[2 * n + 1] = total[:, BLK:F]
        else:
            qsum[2 * n] = qsum[2 * n] + total[:, 0:BLK]
            qsum[2 * n + 1] = qsum[2 * n + 1] + total[:, BLK:F]

    def add_pass(zs_, fresh):
        for n in range(NB // 2):
            add_to(zs_, n, fresh)

    relay = {}
    beside = {}
    onto = {}
    for h in range(2):
        for k in (2, -2):
            one = k // 2
            g[k, h].wait_recv()
            relay[3 * one, h] = send(z - k, xl, h, to_z[one])
            if h == (1 - one) // 2:
                relay[4, h] = send(z - k, xl, h, to_z[k])
            onto[k, h] = send(z - k, xl, h, to_xl)
        g[0, h].wait_recv()
        for k in (1, -1):
            beside[k, h] = send(z, far, h, to_z[k])
    add_pass([z], True)
    for h in range(2):
        for k in (3, -3, 4):
            relay[k, h].wait_recv()
            onto[k, h] = send(z - k, xl, h, to_xl)
    for h in range(2):
        for k in (1, -1):
            g[k, h].wait_recv()
            beside[k, h].wait_recv()
        for k in (2, -2):
            onto[k, h].wait_recv()
    add_pass([z - 1, z + 1, z - 2, z + 2], False)
    for h in range(2):
        for k in (3, -3, 4):
            onto[k, h].wait_recv()

    order = row_moves + [(0, 0)]
    from_sib = []
    sums = []

    def settle(i):
        dy, dx = order[i]
        n = rid(y + dy, swap(xh, dx), 0) // 2
        from_sib[i].wait_recv()
        value = qsum[2 * n + core] + sibr[i]
        if i < 7:
            quant(value, ds.at[i])
            sums.append(push(ds.at[i], dr.at[i], row_devs[i]))
        return value

    for i, (dy, dx) in enumerate(order):
        n = rid(y + dy, swap(xh, dx), 0) // 2
        add_to([z + 3, z - 3, z + 4], n, False)
        from_sib.append(push(qsum.at[2 * n + 1 - core], sibr.at[i], to_sib))
        if i >= 2:
            settle(i - 2)
    settle(6)
    total = settle(7)
    for i in (5, 6, 4, 3, 1, 2, 0):
        sums[i].wait_recv()
        total = total + dequant(dr.at[i])
    gfeat[0] = total.T

    for c in copies:
        c.wait_send()


def body(features, weight, cotangent, block_vals, block_slots, block_count):
    vm = pl.BlockSpec(memory_space=pltpu.VMEM)
    hbm = pl.BlockSpec(memory_space=pl.ANY)
    v = pltpu.VMEM
    coded = (F + 16, BLK)
    small = (BLK + 16, BLK)
    i16 = jnp.int16
    return pl.pallas_call(
        kernel,
        out_shape=(
            jax.ShapeDtypeStruct((BLK, F), BF16),
            jax.ShapeDtypeStruct((1, BLK, F), F32),
        ),
        in_specs=[hbm] * 5 + [pl.BlockSpec(memory_space=pltpu.SMEM)],
        out_specs=(vm, vm),
        scratch_shapes=[
            v((F, F), BF16),
            v((BLK, F), BF16),
            v((1, SLOTS), jnp.int32),
            v((8, NB * NB), jnp.int32),
            pltpu.SMEM((8, NB * NB), jnp.int32),
            v((SLOTS + 1, BLK, BLK), BF16),
            v((NB * BLK, NB * BLK), BF16),
            v((NB * BLK, F), BF16),
            v((8, 2 * BLK, F), F32),
            v((NB, F, BLK), BF16),
            v((NB, F, BLK), F32),
            v((2, 8, *small), i16),
            v((2, 8, *small), i16),
            v((2, 2, *coded), i16),
            v((2, 2, *coded), i16),
            v((2, *small), i16),
            v((2, *small), i16),
            v((2, 2, *small), i16),
            v((2, 2, *small), i16),
            v((2, 2, *small), i16),
            v((2, 2, *small), i16),
            v((8, F, BLK), F32),
            v((7, *coded), i16),
            v((7, *coded), i16),
            pltpu.SemaphoreType.DMA((N_COPIES,)),
            pltpu.SemaphoreType.DMA((N_COPIES,)),
            pltpu.SemaphoreType.DMA((N_LOADS + 6,)),
        ],
        compiler_params=pltpu.CompilerParams(
            collective_id=0, has_side_effects=True, vmem_limit_bytes=56 * 1024 * 1024
        ),
        name="layer",
    )(features, weight, cotangent, block_vals.reshape(SLOTS, BLK, BLK), block_slots, block_count)


def solution(mesh):
    return jax.shard_map(
        body,
        mesh=mesh,
        in_specs=(
            P("col", "row", None),
            P(),
            P(("row", "col"), None),
            P("row", "col", None, None, None),
            P("row", "col", None),
            P("row", "col"),
        ),
        out_specs=(P(("row", "col"), None), P("col", "row", None)),
        check_vma=False,
    )
```

time: 495 us -> 69.7 us (0.14)
  waiting for transfers between devices: 269 us -> 0 us
  matrix products: 110 us -> 0 us
  other arithmetic: 86 us -> 0 us
  Pallas kernels: 0 us -> 65.2 us
  between operations: 13.8 us -> 1.29 us
  local copies, waits for them, and re-layouts: 13.3 us -> 3.04 us
    reduce_scatter x2 -> x0, waiting for transfers between devices: 147 us -> none  [the longest x1 84.2 us: body(): lax.psum_scatter(partial_grad, 'row', scatter_dimension=0, tiled=True)]
    all_gather x2 -> x0, waiting for transfers between devices: 121 us -> none  [the longest x1 65.7 us: body(): strip_rows = lax.all_gather(grad_agg, 'col', axis=0, tiled=True)]
    dot_general x26 -> x0, matrix products: 110 us -> none  [the longest x6 47.8 us: advance(): jnp.einsum('gij,gif->gjf', block_wide, selected_entries, precision=exact_...]
    scatter-add x12 -> x0, other arithmetic: 76.6 us -> none  [advance(): return (running.at[target].add(product, mode='drop'), None)]
    pallas_call x0 -> x1, Pallas kernels: none -> 65.2 us  [body(): pl.pallas_call(kernel, out_shape=(jax.ShapeDtypeStruct((BLK, F), BF16), j...]
    unnamed x12 -> x2, local copies, waits for them, and re-layouts: 12.8 us -> 3.04 us
    select_n x24 -> x0, other arithmetic: 8.1 us -> none  [the longest x12 7.93 us: advance(): return (running.at[target].add(product, mode='drop'), None)]
  transfers between devices with their start and end apart: 4 -> 0, of which waited for: 4 -> 0; matrix products, arithmetic and copies ran while one was open for 2% -> 0% of each run, Pallas kernels for 0% -> 0%
where the time goes in v2:
time: 69.7 us; the launch traced here: 69.5 us
  Pallas kernels  65.2 us (94%)
  local copies, waits for them, and re-layouts  3.04 us (4%)
  between operations  1.29 us (2%)
    pallas_call x1, Pallas kernels, body(): pl.pallas_call(kernel, out_shape=(jax.ShapeDtypeStruct((BLK, F), BF16), j...  65.2 us
    unnamed x2, local copies, waits for them, and re-layouts  3.04 us

profile of v2, /device:TPU:1, one launch (start us, length us, event | category | flops | bytes accessed | tf_op | source)
XLA Modules:
  0.0 69.5 jit_solution(16856549947661830242)
XLA Ops:
  1.3 65.2 %layer.1 = (bf16[128,256]{1,0:T(8,128)(2,1)}, f32[1,128,256]{2,1,0:T(8,128)}) custom-call(bf16[1,128,256]{2,1,0:T(8,128)(2,1)} %feat_hbm.1, bf16[256,256]{1,0:T(8,128)(2,1)} %weight_hbm.1, bf16[128,256]{1,0:T(8,128)(2,1)} %cot_hbm.1, bf16[192,128,128]{2,1,0:T(8,128)(2,1)} %bitcast.1, s32[1,1,192]{2,1,0:T(1,128)} %slots_hbm.1, s32[1,1]{1,0:T(1,128)S(6)} %copy.10.count), custom_call_target="tpu_custom_call" | custom-call | tf_op jit(solution)/shard_map/layer/pallas_call | solution.py:330
  66.5 1.5 %copy.11 = bf16[128,256]{1,0:T(8,128)(2,1)} copy(bf16[128,256]{1,0:T(8,128)(2,1)} %get-tuple-element.4) | data formatting | bytes 131072
  67.9 1.6 %copy.12 = f32[1,128,256]{2,1,0:T(8,128)} copy(f32[1,128,256]{2,1,0:T(8,128)} %get-tuple-element.5) | data formatting | bytes 262144

commit v3 on v2

--- a/solution.py
+++ b/solution.py
@@ -15,7 +15,7 @@
 F32 = jnp.float32
 BF16 = jnp.bfloat16
 LEVELS = 32700.0
-N_COPIES = 96
+N_COPIES = 128
 N_LOADS = 4
 ROOT = 0.7978845608028654
 
@@ -44,9 +44,9 @@
 
 
 def kernel(
-    feat_hbm, weight_hbm, cot_hbm, vals_hbm, slots_hbm, count,
+    feat_hbm, weight_hbm, cot_hbm, vals_hbm, slots_hbm, count_hbm,
     act, gfeat,
-    weight, cot, slots, inv_v, inv, vals, dense, xall, part, gt, qsum,
+    weight, cot, slots, count, inv_v, inv, vals, dense, xall, part, gt, qsum,
     xs, xr, ns, nr, fs, fr, ms, mr, es, er, sibr, ds, dr,
     send_sem, recv_sem, load_sem,
 ):
@@ -89,8 +89,10 @@
     for dev in row_devs + z_devs + [to_sib, to_xl]:
         pl.semaphore_signal(barrier, inc=1, device_id=dev, device_id_type=MESH)
 
-    def xat(r):
-        return xall.at[pl.ds(pl.multiple_of(r * BLK, BLK), BLK)]
+    half = [slice(0, BLK), slice(BLK, F)]
+
+    def xat(h, r):
+        return xall.at[h, pl.ds(pl.multiple_of(r * BLK, BLK), BLK)]
 
     loads = []
 
@@ -99,31 +101,38 @@
         c.start()
         loads.append(c)
 
-    load(feat_hbm.at[0], xat(row))
+    for h in range(2):
+        load(feat_hbm.at[0, :, half[h]], xat(h, row))
     load(slots_hbm.at[0], slots)
+    load(count_hbm, count)
     step = SLOTS // N_LOADS
     for i in range(N_LOADS):
         load(vals_hbm.at[pl.ds(i * step, step)], vals.at[pl.ds(i * step, step)])
     load(weight_hbm, weight)
     load(cot_hbm, cot)
     vals[SLOTS] = jnp.zeros((BLK, BLK), BF16)
-    loads[1].wait()
+    loads[2].wait()
+    loads[3].wait()
     place = lax.broadcasted_iota(jnp.int32, (NB * NB, SLOTS), 0)
     ids = lax.broadcasted_iota(jnp.int32, (NB * NB, SLOTS), 1)
-    hit = jnp.where((slots[...] == place) & (ids < count[0, 0]), 1.0, 0.0).astype(BF16)
+    hit = jnp.where((slots[...] == place) & (ids < count[...]), 1.0, 0.0).astype(BF16)
     marks = (SLOTS - lax.broadcasted_iota(jnp.int32, (8, SLOTS), 1)).astype(F32).astype(BF16)
     found = lax.dot_general(marks, hit, (((1,), (1,)), ((), ())), preferred_element_type=F32)
     inv_v[...] = SLOTS - found.astype(jnp.int32)
     to_smem = pltpu.make_async_copy(inv_v, inv, load_sem.at[len(loads)])
     to_smem.start()
     loads[0].wait()
+    loads[1].wait()
     pl.semaphore_wait(barrier, len(row_devs) + len(z_devs) + 2)
 
-    def put(r, dev):
-        return push(xat(r), xat(r), dev)
-
-    feats = [put(row, dev) for dev in row_devs]
-    sib = [put(row, to_sib)]
+    def put(h, r, dev):
+        return push(xat(h, r), xat(h, r), dev)
+
+    feats = []
+    sib = []
+    for h in range(2):
+        feats.append([put(h, row, dev) for dev in row_devs])
+        sib.append([put(h, row, to_sib)])
 
     def build(lo, hi):
         def one(r, carry):
@@ -134,66 +143,83 @@
         lax.fori_loop(lo, hi, one, 0)
 
     to_smem.wait()
-    for c in loads[2:]:
+    for c in loads[4:]:
         c.wait()
     build(0, NB)
-    for i in (5, 6, 4, 3, 1, 2, 0):
-        dy, dx = row_moves[i]
-        feats[i].wait_recv()
-        sib.append(put(rid(y - dy, swap(xh, dx), core), to_sib))
-    for c in sib:
+
+    def hand_over(h):
+        for i in (5, 6, 4, 3, 1, 2, 0):
+            dy, dx = row_moves[i]
+            feats[h][i].wait_recv()
+            sib[h].append(put(h, rid(y - dy, swap(xh, dx), core), to_sib))
+
+    hand_over(0)
+    for c in sib[0]:
         c.wait_recv()
 
     own_rows = pl.ds(pl.multiple_of(xl * BLK, BLK), BLK)
     far_rows = pl.ds(pl.multiple_of((1 - xl) * BLK, BLK), BLK)
     moves = [4, 3, -3, 1, -1, 2, -2, 0]
     to_z = {k: (row, zmod(z + k) * 2 + xl) for k in (1, -1, 2, -2)}
-    half = [slice(0, BLK), slice(BLK, F)]
     x_copy = {}
     near = {}
 
-    def forward(i):
+    def forward(i, h):
         t = zmod(z + moves[i])
-        part[i] = jnp.dot(
-            dense[pl.ds(pl.multiple_of(t * 2 * BLK, 2 * BLK), 2 * BLK), :], xall[...], preferred_element_type=F32
+        part[i, h] = jnp.dot(
+            dense[pl.ds(pl.multiple_of(t * 2 * BLK, 2 * BLK), 2 * BLK), :], xall[h], preferred_element_type=F32
         )
 
     def cross(i, h):
-        quant(part[i, far_rows, half[h]], xs.at[h, i])
+        quant(part[i, h, far_rows, :], xs.at[h, i])
         x_copy[i, h] = push(xs.at[h, i], xr.at[h, i], to_xl)
 
     def joined(i, h):
         x_copy[i, h].wait_recv()
-        return part[i, own_rows, half[h]] + dequant(xr.at[h, i])
+        return part[i, h, own_rows, :] + dequant(xr.at[h, i])
 
     def pass_on(v, src, dst, dev):
         quant(v, src)
         return push(src, dst, dev)
 
-    for i in range(8):
-        forward(i)
-        if i in (3, 4):
-            for h in range(2):
-                near[i - 3, h] = pass_on(part[i, :, half[h]], ns.at[h, i - 3], nr.at[h, i - 3], to_z[moves[i]])
-        elif i < 7:
-            cross(i, 0)
-        if i == 5:
-            cross(0, 1)
-            cross(1, 1)
-    for i in (2, 5, 6):
-        cross(i, 1)
+    def closer(i, h):
+        near[i - 3, h] = pass_on(part[i, h], ns.at[h, i - 3], nr.at[h, i - 3], to_z[moves[i]])
+
     four = {}
     three = {}
-    for h in range(2):
+
+    def outer(h):
         four[h] = pass_on(joined(0, h), fs.at[h], fr.at[h], to_z[2 - 4 * h])
         for k in range(2):
             three[k, h] = pass_on(joined(1 + k, h), ms.at[h, k], mr.at[h, k], to_z[1 - 2 * k])
-        if h == 0:
-            for k in range(4):
-                near[k % 2, k // 2].wait_recv()
-            for q in range(2):
-                part[7, :, half[q]] = part[7, :, half[q]] + dequant(nr.at[q, 0]) + dequant(nr.at[q, 1])
-                cross(7, q)
+
+    for i in (0, 1, 2, 5, 6):
+        forward(i, 0)
+        cross(i, 0)
+    hand_over(1)
+    for i in (3, 4):
+        forward(i, 0)
+        closer(i, 0)
+    for c in sib[1]:
+        c.wait_recv()
+    for i in (0, 1, 2):
+        forward(i, 1)
+        cross(i, 1)
+    outer(0)
+    for i in (5, 6):
+        forward(i, 1)
+        cross(i, 1)
+    forward(7, 0)
+    for i in (3, 4):
+        forward(i, 1)
+        closer(i, 1)
+    outer(1)
+    forward(7, 1)
+    for h in range(2):
+        for k in range(2):
+            near[k, h].wait_recv()
+        part[7, h] = part[7, h] + dequant(nr.at[h, 0]) + dequant(nr.at[h, 1])
+        cross(7, h)
     last = {}
     for h in range(2):
         for k in range(2):
@@ -238,26 +264,23 @@
         for k in (1, -1):
             g[k, h] = send(z, xl, h, to_z[k])
 
-    def product(zz, n):
+    def product(zz, n, h):
         t = zmod(zz)
-        lhs = jnp.concatenate([gt[t * 2], gt[t * 2 + 1]], axis=1)
+        lhs = jnp.concatenate([gt[t * 2, half[h], :], gt[t * 2 + 1, half[h], :]], axis=1)
         rhs = dense[pl.ds(pl.multiple_of(t * 2 * BLK, 2 * BLK), 2 * BLK), pl.ds(pl.multiple_of(n * 2 * BLK, 2 * BLK), 2 * BLK)]
         return jnp.dot(lhs, rhs, preferred_element_type=F32)
 
-    def add_to(zs_, n, fresh):
-        total = product(zs_[0], n)
+    def add_to(zs_, n, h, fresh):
+        total = product(zs_[0], n, h)
         for zz in zs_[1:]:
-            total = total + product(zz, n)
-        if fresh:
-            qsum[2 * n] = total[:, 0:BLK]
-            qsum[2 * n + 1] = total[:, BLK:F]
-        else:
-            qsum[2 * n] = qsum[2 * n] + total[:, 0:BLK]
-            qsum[2 * n + 1] = qsum[2 * n + 1] + total[:, BLK:F]
-
-    def add_pass(zs_, fresh):
+            total = total + product(zz, n, h)
+        for k in range(2):
+            old = 0.0 if fresh else qsum[2 * n + k, half[h], :]
+            qsum[2 * n + k, half[h], :] = old + total[:, half[k]]
+
+    def add_pass(zs_, h, fresh):
         for n in range(NB // 2):
-            add_to(zs_, n, fresh)
+            add_to(zs_, n, h, fresh)
 
     relay = {}
     beside = {}
@@ -273,8 +296,8 @@
         g[0, h].wait_recv()
         for k in (1, -1):
             beside[k, h] = send(z, far, h, to_z[k])
-    add_pass([z], True)
-    for h in range(2):
+    for h in range(2):
+        add_pass([z], h, True)
         for k in (3, -3, 4):
             relay[k, h].wait_recv()
             onto[k, h] = send(z - k, xl, h, to_xl)
@@ -284,67 +307,71 @@
             beside[k, h].wait_recv()
         for k in (2, -2):
             onto[k, h].wait_recv()
-    add_pass([z - 1, z + 1, z - 2, z + 2], False)
+        add_pass([z - 1, z + 1, z - 2, z + 2], h, False)
+
+    order = row_moves + [(0, 0)]
+    from_sib = {}
+    sums = {}
+    total = []
+
+    def settle(i, h):
+        dy, dx = order[i]
+        n = rid(y + dy, swap(xh, dx), 0) // 2
+        from_sib[i, h].wait_recv()
+        value = qsum[2 * n + core, half[h], :] + sibr[i, half[h], :]
+        if i < 7:
+            sums[i, h] = pass_on(value, ds.at[h, i], dr.at[h, i], row_devs[i])
+        return value
+
     for h in range(2):
         for k in (3, -3, 4):
             onto[k, h].wait_recv()
-
-    order = row_moves + [(0, 0)]
-    from_sib = []
-    sums = []
-
-    def settle(i):
-        dy, dx = order[i]
-        n = rid(y + dy, swap(xh, dx), 0) // 2
-        from_sib[i].wait_recv()
-        value = qsum[2 * n + core] + sibr[i]
-        if i < 7:
-            quant(value, ds.at[i])
-            sums.append(push(ds.at[i], dr.at[i], row_devs[i]))
-        return value
-
-    for i, (dy, dx) in enumerate(order):
-        n = rid(y + dy, swap(xh, dx), 0) // 2
-        add_to([z + 3, z - 3, z + 4], n, False)
-        from_sib.append(push(qsum.at[2 * n + 1 - core], sibr.at[i], to_sib))
-        if i >= 2:
-            settle(i - 2)
-    settle(6)
-    total = settle(7)
-    for i in (5, 6, 4, 3, 1, 2, 0):
-        sums[i].wait_recv()
-        total = total + dequant(dr.at[i])
-    gfeat[0] = total.T
+        for i, (dy, dx) in enumerate(order):
+            n = rid(y + dy, swap(xh, dx), 0) // 2
+            add_to([z + 3, z - 3, z + 4], n, h, False)
+            from_sib[i, h] = push(qsum.at[2 * n + 1 - core, half[h]], sibr.at[i, half[h]], to_sib)
+        for i in range(7):
+            settle(i, h)
+        total.append(settle(7, h))
+    for h in range(2):
+        for i in (5, 6, 4, 3, 1, 2, 0):
+            sums[i, h].wait_recv()
+            total[h] = total[h] + dequant(dr.at[h, i])
+        gfeat[0, :, half[h]] = total[h].T
 
     for c in copies:
         c.wait_send()
 
 
+def hand_out(act_in, grad_in, act, grad):
+    act[...] = act_in[...]
+    grad[...] = grad_in[...]
+
+
 def body(features, weight, cotangent, block_vals, block_slots, block_count):
     vm = pl.BlockSpec(memory_space=pltpu.VMEM)
-    hbm = pl.BlockSpec(memory_space=pl.ANY)
+    hbm = pl.BlockSpec(memory_space=pltpu.HBM)
     v = pltpu.VMEM
     coded = (F + 16, BLK)
     small = (BLK + 16, BLK)
     i16 = jnp.int16
-    return pl.pallas_call(
+    shapes = (jax.ShapeDtypeStruct((BLK, F), BF16), jax.ShapeDtypeStruct((1, BLK, F), F32))
+    results = pl.pallas_call(
         kernel,
-        out_shape=(
-            jax.ShapeDtypeStruct((BLK, F), BF16),
-            jax.ShapeDtypeStruct((1, BLK, F), F32),
-        ),
-        in_specs=[hbm] * 5 + [pl.BlockSpec(memory_space=pltpu.SMEM)],
+        out_shape=shapes,
+        in_specs=[hbm] * 6,
         out_specs=(vm, vm),
         scratch_shapes=[
             v((F, F), BF16),
             v((BLK, F), BF16),
             v((1, SLOTS), jnp.int32),
+            v((1, 1), jnp.int32),
             v((8, NB * NB), jnp.int32),
             pltpu.SMEM((8, NB * NB), jnp.int32),
             v((SLOTS + 1, BLK, BLK), BF16),
             v((NB * BLK, NB * BLK), BF16),
-            v((NB * BLK, F), BF16),
-            v((8, 2 * BLK, F), F32),
+            v((2, NB * BLK, BLK), BF16),
+            v((8, 2, 2 * BLK, BLK), F32),
             v((NB, F, BLK), BF16),
             v((NB, F, BLK), F32),
             v((2, 8, *small), i16),
@@ -358,17 +385,24 @@
             v((2, 2, *small), i16),
             v((2, 2, *small), i16),
             v((8, F, BLK), F32),
-            v((7, *coded), i16),
-            v((7, *coded), i16),
+            v((2, 7, *small), i16),
+            v((2, 7, *small), i16),
             pltpu.SemaphoreType.DMA((N_COPIES,)),
             pltpu.SemaphoreType.DMA((N_COPIES,)),
-            pltpu.SemaphoreType.DMA((N_LOADS + 6,)),
+            pltpu.SemaphoreType.DMA((N_LOADS + 7,)),
         ],
         compiler_params=pltpu.CompilerParams(
             collective_id=0, has_side_effects=True, vmem_limit_bytes=56 * 1024 * 1024
         ),
         name="layer",
     )(features, weight, cotangent, block_vals.reshape(SLOTS, BLK, BLK), block_slots, block_count)
+    return pl.pallas_call(
+        hand_out,
+        out_shape=shapes,
+        in_specs=[vm] * 2,
+        out_specs=(vm, vm),
+        name="hand_out",
+    )(*results)
 
 
 def solution(mesh):

time: 69.7 us -> 65.7 us (0.943)
  local copies, waits for them, and re-layouts: 3.04 us -> 0 us
  Pallas kernels: 65.2 us -> 64.3 us
    unnamed x2 -> x0, local copies, waits for them, and re-layouts: 3.04 us -> none
    pallas_call x1 -> x2, Pallas kernels: 65.2 us -> 64.3 us  [the longest x1 62.7 us: body(): pl.pallas_call(kernel, out_shape=shapes, in_specs=[hbm] * 6, out_specs=(v...]
where the time goes in v3:
time: 65.7 us; the launch traced here: 65.6 us
  Pallas kernels  64.3 us (98%)
  between operations  1.29 us (2%)
    pallas_call x1, Pallas kernels, body(): pl.pallas_call(kernel, out_shape=shapes, in_specs=[hbm] * 6, out_specs=(v...  62.7 us
    pallas_call x1, Pallas kernels, body(): pl.pallas_call(hand_out, out_shape=shapes, in_specs=[vm] * 2, out_specs=(...  1.63 us

profile of v3, /device:TPU:1, one launch (start us, length us, event | category | flops | bytes accessed | tf_op | source)
XLA Modules:
  0.0 65.6 jit_solution(475742328803581668)
XLA Ops:
  1.3 62.7 %layer.1 = (bf16[128,256]{1,0:T(8,128)(2,1)}, f32[1,128,256]{2,1,0:T(8,128)}) custom-call(bf16[1,128,256]{2,1,0:T(8,128)(2,1)} %feat_hbm.1, bf16[256,256]{1,0:T(8,128)(2,1)} %weight_hbm.1, bf16[128,256]{1,0:T(8,128)(2,1)} %cot_hbm.1, bf16[192,128,128]{2,1,0:T(8,128)(2,1)} %bitcast.1, s32[1,1,192]{2,1,0:T(1,128)} %slots_hbm.1, s32[1,1]{1,0:T(1,128)S(6)} %copy.8.count_hbm), custom_call_target="tpu_custom_call" | custom-call | tf_op jit(solution)/shard_map/layer/pallas_call | solution.py:359
  64.0 1.6 %hand_out.1 = (bf16[128,256]{1,0:T(8,128)(2,1)}, f32[1,128,256]{2,1,0:T(8,128)}) custom-call(bf16[128,256]{1,0:T(8,128)(2,1)} %get-tuple-element.4.act_in, f32[1,128,256]{2,1,0:T(8,128)} %get-tuple-element.5.grad_in), custom_call_target="tpu_custom_call" | custom-call | tf_op jit(solution)/shard_map/hand_out/pallas_call | solution.py:399
